TPU v7x, 32 devices: a whole 2x2x4 slice. The times are simulated.
32 devices in a mesh: groups: 2 (over y), seq: 4 (over z), dp: 2 (over x), head: 2 (over core).
Axes of the slice: x: 2, y: 2, z: 4, core: 2. Of those that a mesh axis runs over, the one named last changes fastest.
Arguments:
- latents: bfloat16 [4, 8, 512, 1024], P(('groups', 'dp'), None, 'seq', 'head'), parts along dimension 0, may hold values from -6 to 6
- log_decay: bfloat16 [4, 8, 512, 8], P(('groups', 'dp'), None, 'seq', 'head'), parts along dimension 0, may hold values from -1 to 0, as said below
- seg_lengths: int32 [4, 4], P(('groups', 'dp')), parts along dimension 0, may hold values from 1 to 2048, 4096 in all within a row
- qkv_weight: bfloat16 [1024, 3, 1024], P('seq', None, 'head'), may hold values from -0.1875 to 0.1875
- out_weight: bfloat16 [1024, 1024], P('seq', 'head'), may hold values from -0.1875 to 0.1875
- cotangent: bfloat16 [4, 8, 512, 1024], P(('groups', 'dp'), 'seq', None, 'head'), parts along dimension 0, may hold values from -6 to 6
Outputs:
- layer_out: bfloat16 [4, 8, 512, 1024], P(('groups', 'dp'), 'seq', None, 'head'), parts along dimension 0
- output_weight_gradient: float32 [2048, 1024], P(('groups', 'seq'), 'head'), parts along dimension 0
There are 2 independent parts, one for each index of `groups`. A program takes and returns all parts, laid end to end along the dimension named above; an argument that names none is the same for every part. Nothing has to cross between parts.
Inputs may be any that keep to these rules, and one draw needn't show every extreme that they name: `log_decay`: never positive. `seg_lengths`: each row sums to 4096; a segment's state is reset at its first token.
All inputs are finite; a program needn't handle non-finite values.
Results may differ from a plain program's by a relative error of at most 0.0073.
Values may be sent and summed in bfloat16 or wider, within the bound.
A program may use at most 64 MiB of HBM per device.

v0:
```python
from functools import partial
import jax
import jax.numpy as jnp
from jax import lax
from jax.sharding import PartitionSpec as P


def shifted(value, axis, steps):
    count = lax.axis_size(axis)
    initial, last = (max(0, -steps), min(count, count - steps))
    return lax.ppermute(value, axis, [(source, source + steps) for source in range(initial, last)])


def block_step(carry_state, queries, key_rows, values_in, log_rates, segment, previous):
    head_scale = queries.shape[-1] ** (-0.5)
    cumulative = jnp.cumsum(log_rates, axis=-1)
    size_here = log_rates.shape[-1]
    order_idx = jnp.arange(size_here)
    allowed = (order_idx[:, None] >= order_idx[None, :]) & (segment[:, None] == segment[None, :])
    spread = cumulative[:, :, None] - cumulative[:, None, :]
    weight = jnp.where(allowed[None], jnp.exp(jnp.where(allowed[None], spread, 0.0)), 0.0)
    scores = jnp.einsum("htd,hsd->hts", queries, key_rows, preferred_element_type=jnp.float32)
    mixing = (scores * head_scale * weight).astype(jnp.bfloat16)
    inner_sum = jnp.einsum("hts,hsd->htd", mixing, values_in, preferred_element_type=jnp.float32)
    kept_mask = (segment == previous).astype(jnp.float32)
    carried = jnp.einsum(
        "htd,hde->hte", queries.astype(jnp.float32), carry_state, precision=lax.Precision.HIGHEST
    )
    result = (
        inner_sum
        + kept_mask[None, :, None] * jnp.exp(cumulative)[:, :, None] * carried * head_scale
    )
    last_seg = segment[-1]
    tail_decay = (
        jnp.exp(cumulative[:, -1:] - cumulative)
        * (segment == last_seg).astype(jnp.float32)[None, :]
    )
    decayed = (key_rows.astype(jnp.float32) * tail_decay[:, :, None]).astype(jnp.bfloat16)
    fresh = jnp.einsum("hsd,hse->hde", decayed, values_in, preferred_element_type=jnp.float32)
    through = jnp.exp(cumulative[:, -1]) * (last_seg == previous).astype(jnp.float32)
    return (through[:, None, None] * carry_state + fresh, result)


def to_blocks(array, count):
    moved = array.reshape((array.shape[0], count, array.shape[1] // count) + array.shape[2:])
    return jnp.moveaxis(moved, 1, 0)


def local_pass(queries, key_rows, values_in, log_rates, segment, before, block_size):
    heads_here, length, head_dim = queries.shape
    count = length // block_size
    seg_blocks = segment.reshape(count, block_size)
    previous = jnp.concatenate([jnp.reshape(before, (1,)), seg_blocks[:-1, -1]])

    def advance(carry_state, slab_in):
        q_blk, k_blk, v_blk, r_blk, s_blk, p_blk = slab_in
        return block_step(carry_state, q_blk, k_blk, v_blk, r_blk, s_blk, p_blk)

    start_state = jnp.zeros((heads_here, head_dim, head_dim), jnp.float32)
    final_state, block_outs = lax.scan(
        advance,
        start_state,
        (
            to_blocks(queries, count),
            to_blocks(key_rows, count),
            to_blocks(values_in, count),
            to_blocks(log_rates, count),
            seg_blocks,
            previous,
        ),
    )
    outputs = jnp.moveaxis(block_outs, 0, 1).reshape(heads_here, length, head_dim)
    return (outputs, final_state)


def local(latents, log_decay, seg_lengths, qkv_weight, out_weight, cotangent):
    strips, rate_strips = (
        lax.all_to_all(latents, "seq", split_axis=1, concat_axis=2, tiled=True),
        lax.all_to_all(log_decay, "seq", split_axis=1, concat_axis=2, tiled=True),
    )
    features = lax.all_gather(strips, "head", axis=3, tiled=True)
    proj_full, out_full = (
        lax.all_gather(qkv_weight, "seq", axis=0, tiled=True),
        lax.all_gather(out_weight, "seq", axis=0, tiled=True),
    )
    drives_here, rows_here, columns, feature_width = features.shape
    tokens_here = rows_here * columns
    heads_here = rate_strips.shape[3]
    head_dim = proj_full.shape[2] // heads_here
    block_size = min(512, tokens_here)
    split_weight = proj_full.reshape(feature_width, 3, heads_here, head_dim)
    projected = jnp.einsum(
        "bsaf,fchd->cbhsad", features, split_weight, preferred_element_type=jnp.float32
    ).astype(jnp.bfloat16)
    projected = projected.reshape(3, drives_here, heads_here, tokens_here, head_dim)
    log_rates = jnp.transpose(rate_strips.astype(jnp.float32), (0, 3, 1, 2)).reshape(
        drives_here, heads_here, tokens_here
    )
    starts = jnp.cumsum(seg_lengths, axis=1) - seg_lengths
    first_pos = lax.axis_index("seq") * tokens_here
    position = first_pos + jnp.arange(tokens_here, dtype=jnp.int32)
    segment = jnp.sum((starts[:, :, None] <= position[None, None, :]).astype(jnp.int32), axis=1) - 1
    before = jnp.sum((starts <= first_pos - 1).astype(jnp.int32), axis=1) - 1
    run_local = jax.vmap(partial(local_pass, block_size=block_size))
    local_out, own_state = run_local(
        projected[0], projected[1], projected[2], log_rates, segment, before
    )
    running = jnp.cumsum(log_rates, axis=2)
    joined_seg = (segment[:, -1] == before).astype(jnp.float32)
    self_decay = jnp.exp(running[:, :, -1]) * joined_seg[:, None]

    def relay(step_index, incoming):
        return shifted(self_decay[:, :, None, None] * incoming + own_state, "seq", 1)

    prefix = lax.fori_loop(0, lax.axis_size("seq") - 1, relay, jnp.zeros_like(own_state))
    head_scale = head_dim ** (-0.5)
    kept_mask = (segment == before[:, None]).astype(jnp.float32)
    carried = jnp.einsum(
        "bhtd,bhde->bhte", projected[0].astype(jnp.float32), prefix, precision=lax.Precision.HIGHEST
    )
    combined = (
        local_out
        + kept_mask[:, None, :, None] * jnp.exp(running)[:, :, :, None] * head_scale * carried
    )
    normed = combined * lax.rsqrt(jnp.mean(combined * combined, axis=-1, keepdims=True) + 1e-06)
    attn_rows = jnp.transpose(normed.astype(jnp.bfloat16), (0, 2, 1, 3)).reshape(
        drives_here * tokens_here, heads_here * head_dim
    )
    attn_full = lax.all_gather(attn_rows, "head", axis=1, tiled=True)
    layer_out = jnp.dot(attn_full, out_full, preferred_element_type=jnp.float32).astype(
        jnp.bfloat16
    )
    layer_out = layer_out.reshape(drives_here, rows_here, columns, out_full.shape[1])
    cot_rows = cotangent.reshape(drives_here * tokens_here, cotangent.shape[3])
    factor = float(lax.axis_size("dp") * lax.axis_size("seq") * drives_here * tokens_here) ** (-0.5)
    my_rows = lax.psum_scatter(
        lax.dot_general(
            attn_full, cot_rows, (((0,), (0,)), ((), ())), preferred_element_type=jnp.float32
        )
        * factor,
        "seq",
        scatter_dimension=0,
        tiled=True,
    )
    weight_grad = lax.psum(my_rows, "dp")
    return (layer_out, weight_grad)


def solution(mesh):
    in_specs = (
        P(("groups", "dp"), None, "seq", "head"),
        P(("groups", "dp"), None, "seq", "head"),
        P(("groups", "dp"), None),
        P("seq", None, "head"),
        P("seq", "head"),
        P(("groups", "dp"), "seq", None, "head"),
    )
    out_specs = (P(("groups", "dp"), "seq", None, "head"), P(("groups", "seq"), "head"))
    return jax.shard_map(local, mesh=mesh, in_specs=in_specs, out_specs=out_specs, check_vma=False)
```

profile of v0, /device:TPU:0, one launch (start us, length us, event | category | flops | bytes accessed | tf_op | source)
XLA Modules:
  0.0 310.2 jit_solution(2354458996665151048)
XLA Ops:
  7.2 0.7 all-gather.5.cloned.1.call-update
  8.0 56.2 %all_to_all.27 = bf16[1,8,128,512]{3,2,0,1:T(8,128)(2,1)S(1)} all-to-all(bf16[1,8,128,512]{3,2,0,1:T(8,128)(2,1)} %bitcast.208), channel_id=1, replica_groups=mesh['groups'=2,'seq'=4,'dp'=2,'head'=2] {'seq'}, dimensions={1} | all-to-all | bytes 2097152 | tf_op jit(solution)/shard_map/all_to_all | solution.py:78
  64.1 1.1 copy.67
  65.2 5.1 %all-to-all-start = ((bf16[1,8,128,4]{2,3,0,1:T(4,128)(2,1)}), bf16[1,8,128,4]{2,3,0,1:T(4,128)(2,1)S(1)}, u32[]{:S(2)}, u32[]{:S(2)}) async-start(bf16[1,8,128,4]{2,3,0,1:T(4,128)(2,1)} %bitcast.1), calls=%async_computation | async-start | bytes 16384 | tf_op jit(solution)/shard_map/all_to_all | solution.py:79
  70.5 0.6 fusion.38
  71.3 0.7 slice.57
  72.6 0.8 add_bitcast_fusion
  74.6 1.4 all-to-all-done
  76.0 1.1 reduce-window.16
  78.1 13.0 %all-gather.5.cloned.1.call-done = bf16[1024,3,512]{2,0,1:T(8,128)(2,1)} async-done(((bf16[256,3,512]{2,0,1:T(8,128)(2,1)}), bf16[1024,3,512]{2,0,1:T(8,128)(2,1)}) %all-gather.5.cloned.1.call-update) | async-done | bytes 3145744 | tf_op jit(solution)/shard_map/all_gather | solution.py:83
  91.1 4.7 %copy.65 = bf16[1024,3,512]{0,2,1:T(8,128)(2,1)} copy(bf16[1024,3,512]{2,0,1:T(8,128)(2,1)} %all-gather.5.cloned.1.call-done) | data formatting | bytes 6291456 | tf_op jit(solution)/shard_map/all_gather | solution.py:83
  95.8 7.3 %all-gather.7.cloned.1.call-done = bf16[1,2,512,1024]{3,2,1,0:T(8,128)(2,1)} async-done(((bf16[1,2,512,512]{3,2,1,0:T(8,128)(2,1)}), bf16[1,2,512,1024]{3,2,1,0:T(8,128)(2,1)}) %all-gather.7.cloned.1.call-update) | async-done | bytes 2097168 | tf_op jit(solution)/shard_map/all_gather | solution.py:81
  103.1 6.1 %convert_bitcast_fusion = bf16[3,1,4,2,512,128]{4,5,3,2,0,1:T(8,128)(2,1)S(1)} fusion(bf16[1024,3,4,128,1]{0,3,4,2,1:T(8,128)(2,1)} %bitcast.204, bf16[1,2,512,1024]{3,2,1,0:T(8,128)(2,1)} %all-gather.7.cloned.1.call-done), kind=kOutput, calls=%fused_computation.48 | convolution fusion | flops 3222798336 | bytes 8388608 | tf_op jit(solution)/shard_map/bsaf,fchd->cbhsad/dot_general | solution.py:92
  109.2 2.2 fusion.41
  111.4 29.2 %while.24 = (s32[]{:T(128)}, f32[1,4,128,128]{3,2,1,0:T(8,128)S(1)}, f32[2,1,4,512,128]{4,3,2,1,0:T(8,128)}, f32[2,1,4,512]{3,2,1,0:T(4,128)S(1)}, s32[2,1,512]{...) while((s32[]{:T(128)}, ...), condition=%wide.region_6.7_spmd.clone, body=%wide.region_3.6_spmd.clone.sunk | while | flops 1015816256 | bytes 14092170 | solution.py:60
  112.5 1.2 reduce-window.26
  114.6 3.5 %fusion.69 = f32[4,512,128]{2,1,0:T(8,128)S(1)} fusion(f32[4,512]{1,0:T(4,128)S(1)} %get-tuple-element.263, pred[512,512]{1,0:T(8,128)(4,1)S(1)} %fusion.68, bf16[2,1,4,512,128]{3,4,0,2,1:T(8,128)(2,1)} %get-tuple-element.299, s32[]{:T(128)} %get-tuple-element.279, bf16[2,1,4,512,128]{3,4,0,2,1:T(8,128)(2,1)} %get-tuple-element.298, ...), kind=kOutput, calls=%fused_computation.2.clone.1 | convolution fusion | flops 543162368 | bytes 2901504 | tf_op jit(solution)/shard_map/vmap()/while/body/eval_jaxpr/hts,hsd->htd/dot_general | solution.py:24
  118.1 2.8 fusion.70
  121.0 0.6 slice.92
  122.9 0.6 compare_convert_fusion.7
  123.6 1.1 constant_dynamic-slice_fusion.10
  125.0 0.9 fusion.67
  127.2 1.2 reduce-window.26
  129.2 3.5 %fusion.69 = f32[4,512,128]{2,1,0:T(8,128)S(1)} fusion(f32[4,512]{1,0:T(4,128)S(1)} %get-tuple-element.263, pred[512,512]{1,0:T(8,128)(4,1)S(1)} %fusion.68, bf16[2,1,4,512,128]{3,4,0,2,1:T(8,128)(2,1)} %get-tuple-element.299, s32[]{:T(128)} %get-tuple-element.279, bf16[2,1,4,512,128]{3,4,0,2,1:T(8,128)(2,1)} %get-tuple-element.298, ...), kind=kOutput, calls=%fused_computation.2.clone.1 | convolution fusion | flops 543162368 | bytes 2901504 | tf_op jit(solution)/shard_map/vmap()/while/body/eval_jaxpr/hts,hsd->htd/dot_general | solution.py:24
  132.7 2.8 fusion.70
  135.5 0.6 slice.92
  137.5 0.6 compare_convert_fusion.7
  138.2 1.1 constant_dynamic-slice_fusion.10
  139.6 0.9 fusion.67
  140.5 2.9 copy.72
  143.4 2.9 reshape.615
  146.3 1.6 copy.76
  147.9 28.2 %while.23 = (s32[]{:T(128)}, f32[1,4,128,128]{3,2,1,0:T(8,128)S(1)}, f32[1,4]{1,0:T(1,128)S(1)}, f32[1,4,128,128]{3,2,1,0:T(8,128)S(1)}, s32[]{:T(128)}) while((s32[]{:T(128)}, f32[1,4,128,128]{3,2,1,0:T(8,128)S(1)}, f32[1,4]{1,0:T(1,128)S(1)}, f32[1,4,128,128]{3,2,1,0:T(8,128)S(1)}, s32[]{:T(128)}) %tuple.57), condition=%wide.region_10.11_spmd, body=%wide.region_9.10_spmd.sunk | while | flops 131074 | bytes 1835125 | solution.py:115
  148.0 3.7 %collective-permute-start = (f32[1,4,128,128]{3,2,1,0:T(8,128)S(1)}, f32[1,4,128,128]{3,2,1,0:T(8,128)S(1)}, u32[]{:S(2)}, u32[]{:S(2)}) collective-permute-start(f32[1,4,128,128]{3,2,1,0:T(8,128)S(1)} %multiply_add_fusion.3), channel_id=1, source_target_pairs={{0,4},{4,8},{8,12},{1,5},{5,9},{9,13},{2,6},{6,10},{10,14},{3,7},{... | collective-permute-start | bytes 786440 | tf_op jit(solution)/shard_map/while/body/eval_jaxpr/ppermute | solution.py:11
  151.7 6.0 %collective-permute-done = f32[1,4,128,128]{3,2,1,0:T(8,128)S(1)} collective-permute-done((f32[1,4,128,128]{3,2,1,0:T(8,128)S(1)}, f32[1,4,128,128]{3,2,1,0:T(8,128)S(1)}, u32[]{:S(2)}, u32[]{:S(2)}) %collective-permute-start) | collective-permute-done | bytes 262176 | tf_op jit(solution)/shard_map/while/body/eval_jaxpr/ppermute | solution.py:11
  157.8 4.4 %collective-permute-start = (f32[1,4,128,128]{3,2,1,0:T(8,128)S(1)}, f32[1,4,128,128]{3,2,1,0:T(8,128)S(1)}, u32[]{:S(2)}, u32[]{:S(2)}) collective-permute-start(f32[1,4,128,128]{3,2,1,0:T(8,128)S(1)} %multiply_add_fusion.3), channel_id=1, source_target_pairs={{0,4},{4,8},{8,12},{1,5},{5,9},{9,13},{2,6},{6,10},{10,14},{3,7},{... | collective-permute-start | bytes 786440 | tf_op jit(solution)/shard_map/while/body/eval_jaxpr/ppermute | solution.py:11
  162.2 5.2 %collective-permute-done = f32[1,4,128,128]{3,2,1,0:T(8,128)S(1)} collective-permute-done((f32[1,4,128,128]{3,2,1,0:T(8,128)S(1)}, f32[1,4,128,128]{3,2,1,0:T(8,128)S(1)}, u32[]{:S(2)}, u32[]{:S(2)}) %collective-permute-start) | collective-permute-done | bytes 262176 | tf_op jit(solution)/shard_map/while/body/eval_jaxpr/ppermute | solution.py:11
  167.5 4.4 %collective-permute-start = (f32[1,4,128,128]{3,2,1,0:T(8,128)S(1)}, f32[1,4,128,128]{3,2,1,0:T(8,128)S(1)}, u32[]{:S(2)}, u32[]{:S(2)}) collective-permute-start(f32[1,4,128,128]{3,2,1,0:T(8,128)S(1)} %multiply_add_fusion.3), channel_id=1, source_target_pairs={{0,4},{4,8},{8,12},{1,5},{5,9},{9,13},{2,6},{6,10},{10,14},{3,7},{... | collective-permute-start | bytes 786440 | tf_op jit(solution)/shard_map/while/body/eval_jaxpr/ppermute | solution.py:11
  171.9 4.3 %collective-permute-done = f32[1,4,128,128]{3,2,1,0:T(8,128)S(1)} collective-permute-done((f32[1,4,128,128]{3,2,1,0:T(8,128)S(1)}, f32[1,4,128,128]{3,2,1,0:T(8,128)S(1)}, u32[]{:S(2)}, u32[]{:S(2)}) %collective-permute-start) | collective-permute-done | bytes 262176 | tf_op jit(solution)/shard_map/while/body/eval_jaxpr/ppermute | solution.py:11
  176.2 2.9 multiply_reduce_fusion
  179.1 1.2 multiply_convert_fusion.3
  180.4 12.6 %all-gather.9.cloned.1.call-done = bf16[1024,1024]{0,1:T(8,128)(2,1)} async-done(((bf16[1024,512]{0,1:T(8,128)(2,1)}), bf16[1024,1024]{0,1:T(8,128)(2,1)}) %all-gather.9.cloned.1.call-update) | async-done | bytes 2097168 | tf_op jit(solution)/shard_map/all_gather | solution.py:129
  193.0 4.1 %convolution_multiply_fusion.1 = f32[1024,512]{1,0:T(8,128)} fusion(bf16[1024,1024]{0,1:T(8,128)(2,1)} %all-gather.9.cloned.1.call-done, bf16[1024,512]{1,0:T(8,128)(2,1)S(1)} %bitcast.196), kind=kOutput, calls=%fused_computation.53 | convolution fusion | flops 1074266112 | bytes 5242880 | tf_op jit(solution)/shard_map/dot_general | solution.py:137
  197.8 44.5 %reduce-scatter.2.cloned.1.call-done = f32[256,512]{1,0:T(8,128)} async-done(((f32[1024,512]{1,0:T(8,128)}), f32[256,512]{1,0:T(8,128)}) %reduce-scatter.2.cloned.1.call-update) | async-done | bytes 524304 | tf_op jit(solution)/shard_map/reduce_scatter | solution.py:136
  242.4 28.8 %all-gather.11.cloned.1.call-done = bf16[1024,512]{1,0:T(8,128)(2,1)} async-done(((bf16[256,512]{1,0:T(8,128)(2,1)}), bf16[1024,512]{1,0:T(8,128)(2,1)}) %all-gather.11.cloned.1.call-update) | async-done | bytes 1048592 | tf_op jit(solution)/shard_map/all_gather | solution.py:84
  271.1 3.5 %convolution_convert_fusion = bf16[1024,512]{1,0:T(8,128)(2,1)} fusion(bf16[1024,1024]{0,1:T(8,128)(2,1)S(1)} %copy-done.3, bf16[1024,512]{1,0:T(8,128)(2,1)} %all-gather.11.cloned.1.call-done), kind=kOutput, calls=%fused_computation.54 | convolution fusion | flops 1074266112 | bytes 4194304 | tf_op jit(solution)/shard_map/dot_general | solution.py:130
  274.6 26.9 %all-reduce.2.cloned.1.call-done = f32[256,512]{1,0:T(8,128)} async-done(((f32[256,512]{1,0:T(8,128)}), f32[256,512]{1,0:T(8,128)}) %all-reduce.2.cloned.1.call-update) | async-done | bytes 524304 | tf_op jit(solution)/shard_map/psum | solution.py:145
  301.5 1.9 copy.123
  (85 shorter events, 7.9 us)
Async XLA Ops:
  7.2 185.8 %copy-start = (bf16[1,2,512,512]{3,2,1,0:T(8,128)(2,1)S(1)}, bf16[1,2,512,512]{3,2,1,0:T(8,128)(2,1)}, u32[]{:S(2)}) copy-start(bf16[1,2,512,512]{3,2,1,0:T(8,128)(2,1)} %param.15) | copy-start | bytes 3145732
  7.2 83.9 %all-gather.5.cloned.1.call-start = ((), (), s32[]{:S(2)}) async-start(), calls=%async_computation.3 | async-start | bytes 3932160 | tf_op jit(solution)/shard_map/all_gather | solution.py:83
  7.9 95.2 %all-gather.7.cloned.1.call-start = ((), (), s32[]{:S(2)}) async-start(), calls=%async_computation.4 | async-start | bytes 3145728 | tf_op jit(solution)/shard_map/all_gather | solution.py:81
  64.1 6.2 %copy-start.2 = (s32[1,4]{1,0:T(1,128)S(1)}, s32[1,4]{1,0:T(1,128)}, u32[]{:S(2)}) copy-start(s32[1,4]{1,0:T(1,128)} %param.12) | copy-start | bytes 52
  65.2 10.7 %all-to-all-start = ((bf16[1,8,128,4]{2,3,0,1:T(4,128)(2,1)}), bf16[1,8,128,4]{2,3,0,1:T(4,128)(2,1)S(1)}, u32[]{:S(2)}, u32[]{:S(2)}) async-start(bf16[1,8,128,4]{2,3,0,1:T(4,128)(2,1)} %bitcast.1), calls=%async_computation | async-start | bytes 16384 | tf_op jit(solution)/shard_map/all_to_all | solution.py:79
  70.4 122.6 %all-gather.9.cloned.1.call-start = ((), (), s32[]{:S(2)}) async-start(), calls=%async_computation.5 | async-start | bytes 3145728 | tf_op jit(solution)/shard_map/all_gather | solution.py:129
  120.9 4.1 %copy-start.1 = (bf16[2,1,4,512,128]{3,4,0,2,1:T(8,128)(2,1)S(1)}, bf16[2,1,4,512,128]{3,4,0,2,1:T(8,128)(2,1)}, u32[]{:S(2)}) copy-start(bf16[2,1,4,512,128]{3,4,0,2,1:T(8,128)(2,1)} %get-tuple-element.298) | copy-start | bytes 3145732 | tf_op jit(solution)/shard_map/vmap()/while
  135.5 4.1 %copy-start.1 = (bf16[2,1,4,512,128]{3,4,0,2,1:T(8,128)(2,1)S(1)}, bf16[2,1,4,512,128]{3,4,0,2,1:T(8,128)(2,1)}, u32[]{:S(2)}) copy-start(bf16[2,1,4,512,128]{3,4,0,2,1:T(8,128)(2,1)} %get-tuple-element.298) | copy-start | bytes 3145732 | tf_op jit(solution)/shard_map/vmap()/while
  148.0 9.7 %collective-permute-start = (f32[1,4,128,128]{3,2,1,0:T(8,128)S(1)}, f32[1,4,128,128]{3,2,1,0:T(8,128)S(1)}, u32[]{:S(2)}, u32[]{:S(2)}) collective-permute-start(f32[1,4,128,128]{3,2,1,0:T(8,128)S(1)} %multiply_add_fusion.3), channel_id=1, source_target_pairs={{0,4},{4,8},{8,12},{1,5},{5,9},{9,13},{2,6},{6,10},{10,14},{3,7},{... | collective-permute-start | bytes 786440 | tf_op jit(solution)/shard_map/while/body/eval_jaxpr/ppermute | solution.py:11
  157.8 9.6 %collective-permute-start = (f32[1,4,128,128]{3,2,1,0:T(8,128)S(1)}, f32[1,4,128,128]{3,2,1,0:T(8,128)S(1)}, u32[]{:S(2)}, u32[]{:S(2)}) collective-permute-start(f32[1,4,128,128]{3,2,1,0:T(8,128)S(1)} %multiply_add_fusion.3), channel_id=1, source_target_pairs={{0,4},{4,8},{8,12},{1,5},{5,9},{9,13},{2,6},{6,10},{10,14},{3,7},{... | collective-permute-start | bytes 786440 | tf_op jit(solution)/shard_map/while/body/eval_jaxpr/ppermute | solution.py:11
  167.5 8.7 %collective-permute-start = (f32[1,4,128,128]{3,2,1,0:T(8,128)S(1)}, f32[1,4,128,128]{3,2,1,0:T(8,128)S(1)}, u32[]{:S(2)}, u32[]{:S(2)}) collective-permute-start(f32[1,4,128,128]{3,2,1,0:T(8,128)S(1)} %multiply_add_fusion.3), channel_id=1, source_target_pairs={{0,4},{4,8},{8,12},{1,5},{5,9},{9,13},{2,6},{6,10},{10,14},{3,7},{... | collective-permute-start | bytes 786440 | tf_op jit(solution)/shard_map/while/body/eval_jaxpr/ppermute | solution.py:11
  180.3 62.0 %reduce-scatter.2.cloned.1.call-start = ((), (), s32[]{:S(2)}) async-start(), calls=%async_computation.7 | async-start | bytes 2621440 | tf_op jit(solution)/shard_map/reduce_scatter | solution.py:136
  197.1 74.0 %copy-start.3 = (bf16[1024,1024]{0,1:T(8,128)(2,1)S(1)}, bf16[1024,1024]{0,1:T(8,128)(2,1)}, u32[]{:S(2)}) copy-start(bf16[1024,1024]{0,1:T(8,128)(2,1)} %all-gather.9.cloned.1.call-done) | copy-start | bytes 6291460
  197.1 74.0 %all-gather.11.cloned.1.call-start = ((), (), s32[]{:S(2)}) async-start(), calls=%async_computation.6 | async-start | bytes 1310720 | tf_op jit(solution)/shard_map/all_gather | solution.py:84
  197.7 103.8 %all-reduce.2.cloned.1.call-start = ((), (), s32[]{:S(2)}) async-start(), calls=%async_computation.8 | async-start | bytes 1048576 | tf_op jit(solution)/shard_map/psum | solution.py:145
Sparse Core Ops, SparseCore 0:
  9.6 81.4 all-gather.4
  93.2 9.8 all-gather.6
  180.5 12.4 all-gather.8
  197.3 45.0 reduce-scatter.1
  243.8 27.2 all-gather.10
  273.4 28.0 all-reduce.1
where the time goes:
time: 311 us; the launch traced here: 310 us
  waiting for transfers between devices  151 us (49%)
  blocking collectives  56.2 us (18%)
  matrix products  31.1 us (10%)
  local copies, waits for them, and re-layouts  25.4 us (8%)
  starting transfers between devices  17.8 us (6%)
  between operations  15.5 us (5%)
  other arithmetic  10.4 us (3%)
    all_to_all x1, blocking collectives, local(): lax.all_to_all(latents, 'seq', split_axis=1, concat_axis=2, tiled=True)  56.2 us
    reduce_scatter x1, waiting for transfers between devices, local(): lax.psum_scatter(lax.dot_general(attn_full, cot_rows, (((0,), (0,)), ((),...  44.5 us
    all_gather x1, waiting for transfers between devices, local(): lax.all_gather(out_weight, 'seq', axis=0, tiled=True)  28.8 us
    psum x1, waiting for transfers between devices, local(): weight_grad = lax.psum(my_rows, 'dp')  26.9 us
    ppermute x3, waiting for transfers between devices, shifted(): lax.ppermute(value, axis, [(source, source + steps) for source in range(i...  15.4 us
    all_gather x1, waiting for transfers between devices, local(): lax.all_gather(qkv_weight, 'seq', axis=0, tiled=True)  13 us
    all_gather x1, waiting for transfers between devices, local(): attn_full = lax.all_gather(attn_rows, 'head', axis=1, tiled=True)  12.6 us
    ppermute x3, starting transfers between devices, shifted(): lax.ppermute(value, axis, [(source, source + steps) for source in range(i...  12.5 us
  transfers between devices with their start and end apart: 10, of which 10 were waited for; matrix products, arithmetic and copies ran while one was open for 5% of the time, Pallas kernels for 0%

commit v1 on v0

--- a/solution.py
+++ b/solution.py
@@ -3,6 +3,18 @@
 import jax.numpy as jnp
 from jax import lax
 from jax.sharding import PartitionSpec as P
+
+
+def sent_to_each(array, axis, split, join):
+    ways, here = (lax.axis_size(axis), lax.axis_index(axis))
+    width = array.shape[split] // ways
+    turned = jnp.roll(array, -here * width, axis=split)
+    got = [lax.slice_in_dim(turned, 0, width, axis=split)]
+    for far in range(1, ways):
+        sent = lax.slice_in_dim(turned, far * width, (far + 1) * width, axis=split)
+        got.append(lax.ppermute(sent, axis, [(d, (d + far) % ways) for d in range(ways)]))
+    line = jnp.concatenate(got[::-1], axis=join)
+    return jnp.roll(line, (here + 1) * got[0].shape[join], axis=join)
 
 
 def shifted(value, axis, steps):
@@ -76,7 +88,7 @@
 def local(latents, log_decay, seg_lengths, qkv_weight, out_weight, cotangent):
     strips, rate_strips = (
         lax.all_to_all(latents, "seq", split_axis=1, concat_axis=2, tiled=True),
-        lax.all_to_all(log_decay, "seq", split_axis=1, concat_axis=2, tiled=True),
+        sent_to_each(log_decay, "seq", 1, 2),
     )
     features = lax.all_gather(strips, "head", axis=3, tiled=True)
     proj_full, out_full = (

time: 311 us -> 311 us (level)
  blocking collectives: 56.2 us -> 0 us
  waiting for transfers between devices: 151 us -> 201 us
  starting transfers between devices: 17.8 us -> 24 us
    all_to_all x1 -> x0, blocking collectives: 56.2 us -> none  [local(): lax.all_to_all(latents, 'seq', split_axis=1, concat_axis=2, tiled=True)]
    all_to_all x1, waiting for transfers between devices: 1.38 us -> 43.7 us  [local(): lax.all_to_all(latents, 'seq', split_axis=1, concat_axis=2, tiled=True)]
    all_gather x1, waiting for transfers between devices: 13 us -> 20.6 us  [local(): lax.all_gather(qkv_weight, 'seq', axis=0, tiled=True)]
    ppermute x0 -> x3, starting transfers between devices: none -> 5 us  [sent_to_each(): lax.ppermute(sent, axis, [(d, (d + far) % ways) for d in range(ways)])]
  transfers between devices with their start and end apart: 10 -> 13, of which waited for: 10 -> 10; matrix products, arithmetic and copies ran while one was open for 5% -> 5% of each run, Pallas kernels for 0% -> 0%
where the time goes in v1:
time: 311 us; the launch traced here: 310 us
  waiting for transfers between devices  201 us (65%)
  matrix products  31 us (10%)
  local copies, waits for them, and re-layouts  25.3 us (8%)
  starting transfers between devices  24 us (8%)
  between operations  15.5 us (5%)
  other arithmetic  10.3 us (3%)
    reduce_scatter x1, waiting for transfers between devices, local(): lax.psum_scatter(lax.dot_general(attn_full, cot_rows, (((0,), (0,)), ((),...  44.5 us
    all_to_all x1, waiting for transfers between devices, local(): lax.all_to_all(latents, 'seq', split_axis=1, concat_axis=2, tiled=True)  43.7 us
    all_gather x1, waiting for transfers between devices, local(): lax.all_gather(out_weight, 'seq', axis=0, tiled=True)  28.8 us
    psum x1, waiting for transfers between devices, local(): weight_grad = lax.psum(my_rows, 'dp')  26.9 us
    all_gather x1, waiting for transfers between devices, local(): lax.all_gather(qkv_weight, 'seq', axis=0, tiled=True)  20.6 us
    ppermute x3, waiting for transfers between devices, shifted(): lax.ppermute(value, axis, [(source, source + steps) for source in range(i...  15.4 us
    all_gather x1, waiting for transfers between devices, local(): attn_full = lax.all_gather(attn_rows, 'head', axis=1, tiled=True)  12.6 us
    ppermute x3, starting transfers between devices, shifted(): lax.ppermute(value, axis, [(source, source + steps) for source in range(i...  12.5 us
  transfers between devices with their start and end apart: 13, of which 10 were waited for; matrix products, arithmetic and copies ran while one was open for 5% of the time, Pallas kernels for 0%

profile of v1, /device:TPU:0, one launch (start us, length us, event | category | flops | bytes accessed | tf_op | source)
XLA Modules:
  0.0 310.1 jit_solution(9616503013667939298)
XLA Ops:
  7.2 0.7 all-gather.5.cloned.1.call-update
  7.9 6.3 %all-to-all-start = ((bf16[1,8,128,512]{3,2,0,1:T(8,128)(2,1)}), bf16[1,8,128,512]{3,2,0,1:T(8,128)(2,1)S(1)}, u32[]{:S(2)}, u32[]{:S(2)}) async-start(bf16[1,8,128,512]{3,2,0,1:T(8,128)(2,1)} %bitcast.205), calls=%async_computation | async-start | bytes 2097152 | tf_op jit(solution)/shard_map/all_to_all | solution.py:90
  14.3 3.9 %collective-permute-start.1 = (bf16[1,2,128,4]{2,3,0,1:T(4,128)(2,1)S(1)}, bf16[1,2,128,4]{2,3,0,1:T(4,128)(2,1)S(1)}, u32[]{:S(2)}, u32[]{:S(2)}) collective-permute-start(bf16[1,2,128,4]{2,3,0,1:T(4,128)(2,1)S(1)} %get-tuple-element.179), channel_id=1, source_target_pairs={{0,12},{4,0},{8,4},{12,8},{1,13},{5,1},{9,5},{13,9},{2,14},{6,2},{... | collective-permute-start | bytes 6152 | tf_op jit(solution)/shard_map/ppermute | solution.py:15
  18.2 1.1 collective-permute-start.3
  19.5 0.6 fusion.39
  21.5 43.7 %all-to-all-done = bf16[1,8,128,512]{3,2,0,1:T(8,128)(2,1)S(1)} async-done(((bf16[1,8,128,512]{3,2,0,1:T(8,128)(2,1)}), bf16[1,8,128,512]{3,2,0,1:T(8,128)(2,1)S(1)}, u32[]{:S(2)}, u32[]{:S(2)}) %all-to-all-start) | async-done | bytes 1048608 | tf_op jit(solution)/shard_map/all_to_all | solution.py:90
  65.2 1.1 copy.69
  66.4 0.6 add_bitcast_fusion
  68.3 1.1 reduce-window.16
  70.4 20.6 %all-gather.5.cloned.1.call-done = bf16[1024,3,512]{2,0,1:T(8,128)(2,1)} async-done(((bf16[256,3,512]{2,0,1:T(8,128)(2,1)}), bf16[1024,3,512]{2,0,1:T(8,128)(2,1)}) %all-gather.5.cloned.1.call-update) | async-done | bytes 3145744 | tf_op jit(solution)/shard_map/all_gather | solution.py:95
  91.1 4.7 %copy.67 = bf16[1024,3,512]{0,2,1:T(8,128)(2,1)} copy(bf16[1024,3,512]{2,0,1:T(8,128)(2,1)} %all-gather.5.cloned.1.call-done) | data formatting | bytes 6291456 | tf_op jit(solution)/shard_map/all_gather | solution.py:95
  95.8 7.4 %all-gather.7.cloned.1.call-done = bf16[1,2,512,1024]{3,2,1,0:T(8,128)(2,1)} async-done(((bf16[1,2,512,512]{3,2,1,0:T(8,128)(2,1)}), bf16[1,2,512,1024]{3,2,1,0:T(8,128)(2,1)}) %all-gather.7.cloned.1.call-update) | async-done | bytes 2097168 | tf_op jit(solution)/shard_map/all_gather | solution.py:93
  103.2 6.0 %convert_bitcast_fusion = bf16[3,1,4,2,512,128]{4,5,3,2,0,1:T(8,128)(2,1)S(1)} fusion(bf16[1024,3,4,128,1]{0,3,4,2,1:T(8,128)(2,1)} %bitcast.201, bf16[1,2,512,1024]{3,2,1,0:T(8,128)(2,1)} %all-gather.7.cloned.1.call-done), kind=kOutput, calls=%fused_computation.48 | convolution fusion | flops 3222798336 | bytes 8388608 | tf_op jit(solution)/shard_map/bsaf,fchd->cbhsad/dot_general | solution.py:104
  109.2 2.2 fusion.42
  111.4 29.0 %while.24 = (s32[]{:T(128)}, f32[1,4,128,128]{3,2,1,0:T(8,128)S(1)}, f32[2,1,4,512,128]{4,3,2,1,0:T(8,128)}, f32[2,1,4,512]{3,2,1,0:T(4,128)S(1)}, s32[2,1,512]{...) while((s32[]{:T(128)}, ...), condition=%wide.region_6.7_spmd.clone, body=%wide.region_3.6_spmd.clone.sunk | while | flops 1015816256 | bytes 14092170 | solution.py:72
  111.4 0.6 constant_dynamic-slice_fusion.12
  112.0 0.6 compare_convert_fusion.6
  112.7 1.2 reduce-window.26
  114.7 3.5 %fusion.71 = f32[4,512,128]{2,1,0:T(8,128)S(1)} fusion(f32[4,512]{1,0:T(4,128)S(1)} %get-tuple-element.268, pred[512,512]{1,0:T(8,128)(4,1)S(1)} %fusion.70, bf16[2,1,4,512,128]{3,4,0,2,1:T(8,128)(2,1)} %get-tuple-element.304, s32[]{:T(128)} %get-tuple-element.284, bf16[2,1,4,512,128]{3,4,0,2,1:T(8,128)(2,1)} %get-tuple-element.303, ...), kind=kOutput, calls=%fused_computation.2.clone.1 | convolution fusion | flops 543162368 | bytes 2901504 | tf_op jit(solution)/shard_map/vmap()/while/body/eval_jaxpr/hts,hsd->htd/dot_general | solution.py:36
  118.3 2.8 fusion.72
  123.6 1.1 constant_dynamic-slice_fusion.10
  125.0 0.9 fusion.69
  126.0 0.6 constant_dynamic-slice_fusion.12
  126.6 0.6 compare_convert_fusion.6
  127.2 1.2 reduce-window.26
  129.3 3.5 %fusion.71 = f32[4,512,128]{2,1,0:T(8,128)S(1)} fusion(f32[4,512]{1,0:T(4,128)S(1)} %get-tuple-element.268, pred[512,512]{1,0:T(8,128)(4,1)S(1)} %fusion.70, bf16[2,1,4,512,128]{3,4,0,2,1:T(8,128)(2,1)} %get-tuple-element.304, s32[]{:T(128)} %get-tuple-element.284, bf16[2,1,4,512,128]{3,4,0,2,1:T(8,128)(2,1)} %get-tuple-element.303, ...), kind=kOutput, calls=%fused_computation.2.clone.1 | convolution fusion | flops 543162368 | bytes 2901504 | tf_op jit(solution)/shard_map/vmap()/while/body/eval_jaxpr/hts,hsd->htd/dot_general | solution.py:36
  132.8 2.8 fusion.72
  138.1 1.1 constant_dynamic-slice_fusion.10
  139.5 0.9 fusion.69
  140.5 2.9 copy.74
  143.3 2.9 reshape.599
  146.2 1.6 copy.78
  147.8 28.2 %while.23 = (s32[]{:T(128)}, f32[1,4,128,128]{3,2,1,0:T(8,128)S(1)}, f32[1,4]{1,0:T(1,128)S(1)}, f32[1,4,128,128]{3,2,1,0:T(8,128)S(1)}, s32[]{:T(128)}) while((s32[]{:T(128)}, f32[1,4,128,128]{3,2,1,0:T(8,128)S(1)}, f32[1,4]{1,0:T(1,128)S(1)}, f32[1,4,128,128]{3,2,1,0:T(8,128)S(1)}, s32[]{:T(128)}) %tuple.60), condition=%wide.region_10.11_spmd, body=%wide.region_9.10_spmd.sunk | while | flops 131074 | bytes 1835125 | solution.py:127
  148.0 3.7 %collective-permute-start = (f32[1,4,128,128]{3,2,1,0:T(8,128)S(1)}, f32[1,4,128,128]{3,2,1,0:T(8,128)S(1)}, u32[]{:S(2)}, u32[]{:S(2)}) collective-permute-start(f32[1,4,128,128]{3,2,1,0:T(8,128)S(1)} %multiply_add_fusion.3), channel_id=1, source_target_pairs={{0,4},{4,8},{8,12},{1,5},{5,9},{9,13},{2,6},{6,10},{10,14},{3,7},{... | collective-permute-start | bytes 786440 | tf_op jit(solution)/shard_map/while/body/eval_jaxpr/ppermute | solution.py:23
  151.6 6.0 %collective-permute-done = f32[1,4,128,128]{3,2,1,0:T(8,128)S(1)} collective-permute-done((f32[1,4,128,128]{3,2,1,0:T(8,128)S(1)}, f32[1,4,128,128]{3,2,1,0:T(8,128)S(1)}, u32[]{:S(2)}, u32[]{:S(2)}) %collective-permute-start) | collective-permute-done | bytes 262176 | tf_op jit(solution)/shard_map/while/body/eval_jaxpr/ppermute | solution.py:23
  157.7 4.4 %collective-permute-start = (f32[1,4,128,128]{3,2,1,0:T(8,128)S(1)}, f32[1,4,128,128]{3,2,1,0:T(8,128)S(1)}, u32[]{:S(2)}, u32[]{:S(2)}) collective-permute-start(f32[1,4,128,128]{3,2,1,0:T(8,128)S(1)} %multiply_add_fusion.3), channel_id=1, source_target_pairs={{0,4},{4,8},{8,12},{1,5},{5,9},{9,13},{2,6},{6,10},{10,14},{3,7},{... | collective-permute-start | bytes 786440 | tf_op jit(solution)/shard_map/while/body/eval_jaxpr/ppermute | solution.py:23
  162.1 5.2 %collective-permute-done = f32[1,4,128,128]{3,2,1,0:T(8,128)S(1)} collective-permute-done((f32[1,4,128,128]{3,2,1,0:T(8,128)S(1)}, f32[1,4,128,128]{3,2,1,0:T(8,128)S(1)}, u32[]{:S(2)}, u32[]{:S(2)}) %collective-permute-start) | collective-permute-done | bytes 262176 | tf_op jit(solution)/shard_map/while/body/eval_jaxpr/ppermute | solution.py:23
  167.4 4.4 %collective-permute-start = (f32[1,4,128,128]{3,2,1,0:T(8,128)S(1)}, f32[1,4,128,128]{3,2,1,0:T(8,128)S(1)}, u32[]{:S(2)}, u32[]{:S(2)}) collective-permute-start(f32[1,4,128,128]{3,2,1,0:T(8,128)S(1)} %multiply_add_fusion.3), channel_id=1, source_target_pairs={{0,4},{4,8},{8,12},{1,5},{5,9},{9,13},{2,6},{6,10},{10,14},{3,7},{... | collective-permute-start | bytes 786440 | tf_op jit(solution)/shard_map/while/body/eval_jaxpr/ppermute | solution.py:23
  171.8 4.3 %collective-permute-done = f32[1,4,128,128]{3,2,1,0:T(8,128)S(1)} collective-permute-done((f32[1,4,128,128]{3,2,1,0:T(8,128)S(1)}, f32[1,4,128,128]{3,2,1,0:T(8,128)S(1)}, u32[]{:S(2)}, u32[]{:S(2)}) %collective-permute-start) | collective-permute-done | bytes 262176 | tf_op jit(solution)/shard_map/while/body/eval_jaxpr/ppermute | solution.py:23
  176.1 2.9 multiply_reduce_fusion
  179.0 1.2 multiply_convert_fusion.3
  180.3 12.6 %all-gather.9.cloned.1.call-done = bf16[1024,1024]{0,1:T(8,128)(2,1)} async-done(((bf16[1024,512]{0,1:T(8,128)(2,1)}), bf16[1024,1024]{0,1:T(8,128)(2,1)}) %all-gather.9.cloned.1.call-update) | async-done | bytes 2097168 | tf_op jit(solution)/shard_map/all_gather | solution.py:141
  192.9 4.1 %convolution_multiply_fusion.1 = f32[1024,512]{1,0:T(8,128)} fusion(bf16[1024,1024]{0,1:T(8,128)(2,1)} %all-gather.9.cloned.1.call-done, bf16[1024,512]{1,0:T(8,128)(2,1)S(1)} %bitcast.193), kind=kOutput, calls=%fused_computation.53 | convolution fusion | flops 1074266112 | bytes 5242880 | tf_op jit(solution)/shard_map/dot_general | solution.py:149
  197.7 44.5 %reduce-scatter.2.cloned.1.call-done = f32[256,512]{1,0:T(8,128)} async-done(((f32[1024,512]{1,0:T(8,128)}), f32[256,512]{1,0:T(8,128)}) %reduce-scatter.2.cloned.1.call-update) | async-done | bytes 524304 | tf_op jit(solution)/shard_map/reduce_scatter | solution.py:148
  242.3 28.8 %all-gather.11.cloned.1.call-done = bf16[1024,512]{1,0:T(8,128)(2,1)} async-done(((bf16[256,512]{1,0:T(8,128)(2,1)}), bf16[1024,512]{1,0:T(8,128)(2,1)}) %all-gather.11.cloned.1.call-update) | async-done | bytes 1048592 | tf_op jit(solution)/shard_map/all_gather | solution.py:96
  271.0 3.5 %convolution_convert_fusion = bf16[1024,512]{1,0:T(8,128)(2,1)} fusion(bf16[1024,1024]{0,1:T(8,128)(2,1)S(1)} %copy-done.4, bf16[1024,512]{1,0:T(8,128)(2,1)} %all-gather.11.cloned.1.call-done), kind=kOutput, calls=%fused_computation.54 | convolution fusion | flops 1074266112 | bytes 4194304 | tf_op jit(solution)/shard_map/dot_general | solution.py:142
  274.5 26.9 %all-reduce.2.cloned.1.call-done = f32[256,512]{1,0:T(8,128)} async-done(((f32[256,512]{1,0:T(8,128)}), f32[256,512]{1,0:T(8,128)}) %all-reduce.2.cloned.1.call-update) | async-done | bytes 524304 | tf_op jit(solution)/shard_map/psum | solution.py:157
  301.4 1.9 copy.132
  (100 shorter events, 8.5 us)
Async XLA Ops:
  7.2 185.7 %copy-start = (bf16[1,2,512,512]{3,2,1,0:T(8,128)(2,1)S(1)}, bf16[1,2,512,512]{3,2,1,0:T(8,128)(2,1)}, u32[]{:S(2)}) copy-start(bf16[1,2,512,512]{3,2,1,0:T(8,128)(2,1)} %param.15) | copy-start | bytes 3145732
  7.2 7.1 %copy-start.2 = (bf16[1,8,128,4]{2,3,1,0:T(4,128)(2,1)S(1)}, bf16[1,8,128,4]{2,3,1,0:T(4,128)(2,1)}, u32[]{:S(2)}) copy-start(bf16[1,8,128,4]{2,3,1,0:T(4,128)(2,1)} %param.11) | copy-start | bytes 24580
  7.2 12.2 %copy-start.3 = (s32[1,4]{1,0:T(1,128)S(1)}, s32[1,4]{1,0:T(1,128)}, u32[]{:S(2)}) copy-start(s32[1,4]{1,0:T(1,128)} %param.12) | copy-start | bytes 52
  7.2 83.9 %all-gather.5.cloned.1.call-start = ((), (), s32[]{:S(2)}) async-start(), calls=%async_computation.2 | async-start | bytes 3932160 | tf_op jit(solution)/shard_map/all_gather | solution.py:95
  7.9 57.3 %all-to-all-start = ((bf16[1,8,128,512]{3,2,0,1:T(8,128)(2,1)}), bf16[1,8,128,512]{3,2,0,1:T(8,128)(2,1)S(1)}, u32[]{:S(2)}, u32[]{:S(2)}) async-start(bf16[1,8,128,512]{3,2,0,1:T(8,128)(2,1)} %bitcast.205), calls=%async_computation | async-start | bytes 2097152 | tf_op jit(solution)/shard_map/all_to_all | solution.py:90
  14.3 88.9 %all-gather.7.cloned.1.call-start = ((), (), s32[]{:S(2)}) async-start(), calls=%async_computation.3 | async-start | bytes 3145728 | tf_op jit(solution)/shard_map/all_gather | solution.py:93
  14.3 53.8 %collective-permute-start.1 = (bf16[1,2,128,4]{2,3,0,1:T(4,128)(2,1)S(1)}, bf16[1,2,128,4]{2,3,0,1:T(4,128)(2,1)S(1)}, u32[]{:S(2)}, u32[]{:S(2)}) collective-permute-start(bf16[1,2,128,4]{2,3,0,1:T(4,128)(2,1)S(1)} %get-tuple-element.179), channel_id=1, source_target_pairs={{0,12},{4,0},{8,4},{12,8},{1,13},{5,1},{9,5},{13,9},{2,14},{6,2},{... | collective-permute-start | bytes 6152 | tf_op jit(solution)/shard_map/ppermute | solution.py:15
  18.2 49.9 %collective-permute-start.2 = (bf16[1,2,128,4]{2,3,0,1:T(4,128)(2,1)S(1)}, bf16[1,2,128,4]{2,3,0,1:T(4,128)(2,1)S(1)}, u32[]{:S(2)}, u32[]{:S(2)}) collective-permute-start(bf16[1,2,128,4]{2,3,0,1:T(4,128)(2,1)S(1)} %get-tuple-element.178), channel_id=1, source_target_pairs={{0,8},{4,12},{8,0},{12,4},{1,9},{5,13},{9,1},{13,5},{2,10},{6,14},... | collective-permute-start | bytes 6152 | tf_op jit(solution)/shard_map/ppermute | solution.py:15
  18.2 50.0 %collective-permute-start.3 = (bf16[1,2,128,4]{2,3,0,1:T(4,128)(2,1)S(1)}, bf16[1,2,128,4]{2,3,0,1:T(4,128)(2,1)S(1)}, u32[]{:S(2)}, u32[]{:S(2)}) collective-permute-start(bf16[1,2,128,4]{2,3,0,1:T(4,128)(2,1)S(1)} %get-tuple-element.177), channel_id=1, source_target_pairs={{0,4},{4,8},{8,12},{12,0},{1,5},{5,9},{9,13},{13,1},{2,6},{6,10},{... | collective-permute-start | bytes 6152 | tf_op jit(solution)/shard_map/ppermute | solution.py:15
  66.3 126.6 %all-gather.9.cloned.1.call-start = ((), (), s32[]{:S(2)}) async-start(), calls=%async_computation.4 | async-start | bytes 3145728 | tf_op jit(solution)/shard_map/all_gather | solution.py:141
  121.1 3.9 %copy-start.1 = (bf16[2,1,4,512,128]{3,4,0,2,1:T(8,128)(2,1)S(1)}, bf16[2,1,4,512,128]{3,4,0,2,1:T(8,128)(2,1)}, u32[]{:S(2)}) copy-start(bf16[2,1,4,512,128]{3,4,0,2,1:T(8,128)(2,1)} %get-tuple-element.303) | copy-start | bytes 3145732 | tf_op jit(solution)/shard_map/vmap()/while
  135.6 3.9 %copy-start.1 = (bf16[2,1,4,512,128]{3,4,0,2,1:T(8,128)(2,1)S(1)}, bf16[2,1,4,512,128]{3,4,0,2,1:T(8,128)(2,1)}, u32[]{:S(2)}) copy-start(bf16[2,1,4,512,128]{3,4,0,2,1:T(8,128)(2,1)} %get-tuple-element.303) | copy-start | bytes 3145732 | tf_op jit(solution)/shard_map/vmap()/while
  148.0 9.7 %collective-permute-start = (f32[1,4,128,128]{3,2,1,0:T(8,128)S(1)}, f32[1,4,128,128]{3,2,1,0:T(8,128)S(1)}, u32[]{:S(2)}, u32[]{:S(2)}) collective-permute-start(f32[1,4,128,128]{3,2,1,0:T(8,128)S(1)} %multiply_add_fusion.3), channel_id=1, source_target_pairs={{0,4},{4,8},{8,12},{1,5},{5,9},{9,13},{2,6},{6,10},{10,14},{3,7},{... | collective-permute-start | bytes 786440 | tf_op jit(solution)/shard_map/while/body/eval_jaxpr/ppermute | solution.py:23
  157.7 9.6 %collective-permute-start = (f32[1,4,128,128]{3,2,1,0:T(8,128)S(1)}, f32[1,4,128,128]{3,2,1,0:T(8,128)S(1)}, u32[]{:S(2)}, u32[]{:S(2)}) collective-permute-start(f32[1,4,128,128]{3,2,1,0:T(8,128)S(1)} %multiply_add_fusion.3), channel_id=1, source_target_pairs={{0,4},{4,8},{8,12},{1,5},{5,9},{9,13},{2,6},{6,10},{10,14},{3,7},{... | collective-permute-start | bytes 786440 | tf_op jit(solution)/shard_map/while/body/eval_jaxpr/ppermute | solution.py:23
  167.4 8.7 %collective-permute-start = (f32[1,4,128,128]{3,2,1,0:T(8,128)S(1)}, f32[1,4,128,128]{3,2,1,0:T(8,128)S(1)}, u32[]{:S(2)}, u32[]{:S(2)}) collective-permute-start(f32[1,4,128,128]{3,2,1,0:T(8,128)S(1)} %multiply_add_fusion.3), channel_id=1, source_target_pairs={{0,4},{4,8},{8,12},{1,5},{5,9},{9,13},{2,6},{6,10},{10,14},{3,7},{... | collective-permute-start | bytes 786440 | tf_op jit(solution)/shard_map/while/body/eval_jaxpr/ppermute | solution.py:23
  180.2 62.0 %reduce-scatter.2.cloned.1.call-start = ((), (), s32[]{:S(2)}) async-start(), calls=%async_computation.6 | async-start | bytes 2621440 | tf_op jit(solution)/shard_map/reduce_scatter | solution.py:148
  197.0 74.0 %copy-start.4 = (bf16[1024,1024]{0,1:T(8,128)(2,1)S(1)}, bf16[1024,1024]{0,1:T(8,128)(2,1)}, u32[]{:S(2)}) copy-start(bf16[1024,1024]{0,1:T(8,128)(2,1)} %all-gather.9.cloned.1.call-done) | copy-start | bytes 6291460
  197.1 74.0 %all-gather.11.cloned.1.call-start = ((), (), s32[]{:S(2)}) async-start(), calls=%async_computation.5 | async-start | bytes 1310720 | tf_op jit(solution)/shard_map/all_gather | solution.py:96
  197.7 103.8 %all-reduce.2.cloned.1.call-start = ((), (), s32[]{:S(2)}) async-start(), calls=%async_computation.7 | async-start | bytes 1048576 | tf_op jit(solution)/shard_map/psum | solution.py:157
Sparse Core Ops, SparseCore 0:
  9.6 81.4 all-gather.4
  93.2 9.9 all-gather.6
  180.4 12.4 all-gather.8
  197.2 45.0 reduce-scatter.1
  243.7 27.2 all-gather.10
  273.3 28.0 all-reduce.1
